TPU v7x, 128 devices: a whole 4x4x4 slice. The times are simulated.
128 devices in a mesh: pipe: 2 (over x_lo), dp: 32 (over x_hi, z, y), tensor: 2 (over core).
Axes of the slice: x: 4 (x_hi: 2, x_lo: 2; x = x_hi * 2 + x_lo), y: 4, z: 4, core: 2. Of those that a mesh axis runs over, the one named last changes fastest.
Arguments:
- inputs: bfloat16 [2, 4096, 896], P(None, ('dp', 'tensor')), may hold values from -16 to 16
- cotangent: bfloat16 [2, 4096, 896], P(None, ('dp', 'tensor')), may hold values from -16 to 16
- lengths: int32 [2, 32, 4], P(None, 'dp'), may hold values from 0 to 128, as said below
- gain_attn: bfloat16 [2, 896], P('pipe'), may hold values from 0.099609375 to 1.8984375
- w_query: bfloat16 [2, 896, 896], P('pipe', None, 'tensor'), may hold values from -0.1875 to 0.1875
- b_query: bfloat16 [2, 896], P('pipe', 'tensor'), may hold values from -3 to 3
- w_keyval: bfloat16 [2, 896, 2, 128], P('pipe', None, 'tensor'), may hold values from -0.1875 to 0.1875
- b_keyval: bfloat16 [2, 2, 128], P('pipe', 'tensor'), may hold values from -3 to 3
- w_out: bfloat16 [2, 896, 896], P('pipe', 'tensor'), may hold values from -0.75 to 0.75
- gain_mlp: bfloat16 [2, 896], P('pipe'), may hold values from 0.099609375 to 1.8984375
- w_gate_up: bfloat16 [2, 896, 2, 4864], P('pipe', None, None, 'tensor'), may hold values from -0.1875 to 0.1875
- w_down: bfloat16 [2, 4864, 896], P('pipe', 'tensor'), may hold values from -0.078125 to 0.078125
Outputs:
- section_out: bfloat16 [2, 2, 4096, 896], P('pipe', None, ('dp', 'tensor'))
- input_grad: float32 [2, 2, 4096, 896], P('pipe', None, ('dp', 'tensor'))
- grad_gain_attn: float32 [2, 896], P('pipe')
- grad_w_query: float32 [2, 896, 896], P('pipe', 'dp', 'tensor')
- grad_b_query: float32 [2, 896], P('pipe')
- grad_w_keyval: float32 [2, 896, 2, 128], P('pipe', 'dp', 'tensor')
- grad_b_keyval: float32 [2, 2, 128], P('pipe')
- grad_w_out: float32 [2, 896, 896], P('pipe', 'tensor', 'dp')
- grad_gain_mlp: float32 [2, 896], P('pipe')
- grad_w_gate_up: float32 [2, 896, 2, 4864], P('pipe', 'dp', None, 'tensor')
- grad_w_down: float32 [2, 4864, 896], P('pipe', 'tensor', 'dp')
Inputs may be any that keep to these rules, and one draw needn't show every extreme that they name: In every micro-batch the lengths of one rank sum to more than 64 and at most 128; each rank's first sequence is longer than 64; in every micro-batch some rank holds a single sequence of exactly 128; later lengths may be 0.
All inputs are finite; a program needn't handle non-finite values.
Results may differ from a plain program's by a relative error of at most 0.03.
Values may be sent and summed in bfloat16 or wider, within the bound.
A program may use at most 256 MiB of HBM per device.

v0:
```python
import functools

import jax
import jax.numpy as jnp
import numpy as np
from jax import lax
from jax.experimental import pallas as pl
from jax.experimental.pallas import tpu as pltpu
from jax.sharding import PartitionSpec as P

D = 896
HEADS = 14
HEAD = 64
CAP = 128
SEQS = 4
MICRO = 2
ROWS = MICRO * CAP
OWN = CAP // 2
FH = 2432
QW = 448
EPS = 1e-06
THETA = 1000000.0
MIB = 1024 * 1024

BF = jnp.bfloat16
F32 = jnp.float32
MESH = pl.DeviceIdType.MESH
VMEM = pltpu.VMEM

PIECES = {
    "a0": ("down", 0, 640, 0), "a1": ("gate", 0, 896, 640), "a2": ("gate", 896, 1152, 1536),
    "a3": ("out", 0, 512, 2688), "a4": ("qkv", 0, 640, 3200),
    "b0": ("down", 640, 640, 3840), "b1": ("up", 0, 896, 4480), "b2": ("up", 896, 1280, 5376),
    "c0": ("down", 1280, 512, 0), "c1": ("down", 1792, 640, 512), "c2": ("gate", 2048, 384, 1152), "c3": ("up", 2176, 256, 1536),
}
NAMES = tuple(PIECES)
COLS_AB = 6656
COLS_C = 1792
SPLIT = {"c0": 256, "c1": 256, "c2": 256, "c3": 128}
SERVICE = (
    "cx:c0 m0:a0 m0:a1 m0:b0",
    "m0:b1 m0:a2 m0:b2 m0:a3",
    "m0:c0 cx:c1 s:b0 m0:a4",
    "s:b1 cx:c2 s:a0 s:b2",
    "s:a1 s:c0 cx:c3 m0:c1",
    "m0:c2 s:a2 m1:a0 s:a3",
    "m1:a1 m1:b0 m0:c3 s:c1",
    "s:a4 s:c2 m1:b1 m1:a2",
    "m1:b2 t:a0 m1:a3 m1:c0",
    "t:a1 t:b0 e:a0 s:c3",
    "m1:c1 m1:a4 m1:c2 t:b1",
    "e:a1 t:a2 t:a3 e:b0",
    "t:b2 t:c0 m1:c3 t:a4",
    "t:c1 t:c2 e:b1 t:c3",
    "e:a2 e:a3 e:b2 e:a4",
)
SERVICE = tuple(event for line in SERVICE for event in line.split())
TILES = ((0, 512), (512, 512), (1024, 512), (1536, 512), (2048, 384))
WIDE = ((0, 256), (256, 256), (512, 256), (768, 128))


def nn(a, b):
    return lax.dot_general(a, b, (((1,), (0,)), ((), ())), preferred_element_type=F32)


def nt(a, b):
    return lax.dot_general(a, b, (((1,), (1,)), ((), ())), preferred_element_type=F32)


def tn(a, b):
    return lax.dot_general(a, b, (((0,), (0,)), ((), ())), preferred_element_type=F32)


def rope_table():
    half = HEAD // 2
    frequency = np.power(np.float32(THETA), -(np.arange(half, dtype=np.float32) * np.float32(2.0 / HEAD)))
    phases = (np.arange(CAP, dtype=np.float32)[:, None] * frequency[None, :].astype(np.float32)).astype(np.float32)
    phases = phases.astype(np.float64)
    cosine = np.concatenate([np.cos(phases)] * 4, axis=1).astype(np.float32)
    sine = np.concatenate([-np.sin(phases), np.sin(phases)] * 2, axis=1).astype(np.float32)
    parts = []
    for table in (cosine, sine):
        rest = table
        for _ in range(3):
            piece = rest.astype(jnp.bfloat16)
            parts.append(piece)
            rest = rest - piece.astype(np.float32)
    return np.concatenate(parts, axis=1)


def row_order():
    index = np.arange(D)
    y, z, x_hi, k = index // 224, index // 56 % 4, index // 28 % 2, index % 28
    source = (x_hi * 16 + z * 4 + y) * 28 + k
    return (source[:, None] == np.arange(D)[None, :]).astype(jnp.bfloat16)


def turn(block, lane):
    low = (lane & 63) < 32
    return jnp.where(low, pltpu.roll(block, 96, 1), pltpu.roll(block, 32, 1))


def train_kernel(
    len_ref, x_ref, cot_ref, g1_ref, g2_ref, bq_ref, bkv_ref, tab_ref,
    wq_hbm, wkv_hbm, wo_hbm, wgu_hbm, wd_hbm, perm_hbm,
    sums_ref, rows_ref,
    wq, wkv, wo, wgu, wd, perm, xbuf, gbuf, e1s, e1r, e2s, e2r, pipe_out,
    n1, n2, qb, kb, vb, pmat, mix, middle, dgate, dup, hidden, lt, part, gmid, cs, allow, gqkv,
    lt_n, mb_ref, gdown, gout, gqkv_w,
    r1, r2, h2, q1, q2, h3, q3, cx, c1, c2, hc, d1, d2, small_in,
    load_sem, send_sem, recv_sem, sum_send, sum_recv, small_send, small_recv,
):
    pipe = lax.axis_index("pipe")
    t = lax.axis_index("tensor")
    rank = lax.axis_index("dp")
    other = 1 - t
    x_hi, z, y = rank // 16, (rank // 4) % 4, rank % 4
    pos = (y, z)

    loads = [
        pltpu.make_async_copy(wq_hbm, wq.at[pl.ds(0, QW)], load_sem.at[0]),
        pltpu.make_async_copy(wkv_hbm, wkv, load_sem.at[1]),
        pltpu.make_async_copy(wo_hbm, wo.at[pl.ds(0, QW)], load_sem.at[2]),
        pltpu.make_async_copy(wgu_hbm, wgu, load_sem.at[3]),
        pltpu.make_async_copy(wd_hbm, wd, load_sem.at[4]),
        pltpu.make_async_copy(perm_hbm, perm, load_sem.at[5]),
    ]
    for c in loads:
        c.start()

    def to_core(src, dst, i):
        return pltpu.make_async_remote_copy(
            src_ref=src, dst_ref=dst, send_sem=send_sem.at[i], recv_sem=recv_sem.at[i],
            device_id={"tensor": other}, device_id_type=MESH)

    def to_pipe(src, dst, i):
        return pltpu.make_async_remote_copy(
            src_ref=src, dst_ref=dst, send_sem=send_sem.at[i], recv_sem=recv_sem.at[i],
            device_id={"pipe": 1 - pipe}, device_id_type=MESH)

    share_x = to_core(xbuf.at[:, t], xbuf.at[:, t], 0)
    share_g = to_core(gbuf.at[:, t], gbuf.at[:, t], 1)
    pass_x = to_pipe(pipe_out, xbuf.at[:, t], 2)
    pass_g = to_pipe(pipe_out, gbuf.at[:, t], 3)
    swap_1 = to_core(e1s, e1r, 4)
    swap_2 = to_core(e2s, e2r, 5)
    swap_3 = to_core(e1s, e1r, 6)
    swap_4 = to_core(e2s, e2r, 7)

    def at(yy, zz, xx):
        return {"dp": xx * 16 + zz * 4 + yy}

    def along(axis, step):
        if axis == 0:
            return at((y + step) % 4, z, x_hi)
        return at(y, (z + step) % 4, x_hi)

    x_peer = at(y, z, 1 - x_hi)
    peers = [along(0, 1), along(0, 3), along(1, 1), along(1, 3), x_peer, {"tensor": other}, {"pipe": 1 - pipe}]
    barrier = pltpu.get_barrier_semaphore()
    for peer in peers:
        pl.semaphore_signal(barrier, inc=1, device_id=peer, device_id_type=MESH)
    pl.semaphore_wait(barrier, len(peers))

    def remote(src, dst, peer, *sem):
        return pltpu.make_async_remote_copy(
            src_ref=src, dst_ref=dst, send_sem=sum_send.at[sem], recv_sem=sum_recv.at[sem],
            device_id=peer, device_id_type=MESH)

    bufs = {"down": gdown, "gate": wgu.at[0], "up": wgu.at[1], "out": gout, "qkv": gqkv_w}

    def columns(name, half=None):
        _, _, w, c = PIECES[name]
        if half is None:
            return pl.ds(c, w)
        cutoff = SPLIT[name]
        return pl.ds(c, cutoff) if half == 0 else pl.ds(c + cutoff, w - cutoff)

    def held(name, start, count):
        buf, c, w, _ = PIECES[name]
        return bufs[buf].at[pl.ds(pl.multiple_of(start, 16), count), pl.ds(c, w)]

    def ring(name, stage):
        if name[0] == "c":
            here = lambda half: columns(name, half)
            if stage == 0:
                return (1, lambda q, half: cx.at[pl.ds(pl.multiple_of(q * 112, 16), 112), here(half)],
                        lambda half: c1.at[:, here(half)], lambda k, half: c2.at[k, :, here(half)])
            return (0, lambda q, half: hc.at[q, :, here(half)],
                    lambda half: d1.at[:, here(half)], lambda k, half: d2.at[k, :, here(half)])
        axis = "ab".index(name[0])
        cols = columns(name)
        if stage == 0:
            return (axis, lambda q, half: held(name, q * 224 + 112 * half, 112),
                    lambda half: r1.at[half, :, cols], lambda k, half: r2.at[k, half, :, cols])
        return (1 - axis, lambda q, half: h2.at[q, pl.ds(32 * half, 32), cols],
                lambda half: q1.at[half, :, cols], lambda k, half: q2.at[k, half, :, cols])

    def ring_copy(name, stage, k):
        axis, block, first, last = ring(name, stage)
        f = pos[axis]
        ahead, behind = along(axis, 1), along(axis, 3)
        src, dst, peer = (
            lambda: (block((f + 2) % 4, 0), first(0), ahead),
            lambda: (block((f + 2) % 4, 1), first(1), behind),
            lambda: (block((f + 1) % 4, 1), last(0, 1), ahead),
            lambda: (block((f + 3) % 4, 0), last(1, 0), behind),
            lambda: (first(0), last(0, 0), ahead),
            lambda: (first(1), last(1, 1), behind),
        )[k]()
        return remote(src, dst, peer, NAMES.index(name), 6 * stage + k)

    def ring_begin(name, stage):
        for k in range(4):
            ring_copy(name, stage, k).start()

    def ring_middle(name, stage):
        axis, block, first, _ = ring(name, stage)
        f = pos[axis]
        for k, q in enumerate(((f + 1) % 4, (f + 3) % 4)):
            ring_copy(name, stage, k).wait_recv()
            own = block(q, k)[...]
            slot = first(k)
            slot[...] = (own.astype(F32) + slot[...].astype(F32)).astype(BF)
            ring_copy(name, stage, 4 + k).start()

    def ring_total(name, stage):
        axis, block, _, last = ring(name, stage)
        for k in range(2, 6):
            ring_copy(name, stage, k).wait_recv()
        return [
            block(pos[axis], half)[...].astype(F32) + last(0, half)[...].astype(F32) + last(1, half)[...].astype(F32)
            for half in range(2)]

    def x_copy(name):
        if name[0] == "c":
            return remote(held(name, (1 - x_hi) * 448, 448), cx.at[:, columns(name)], x_peer, NAMES.index(name), 12)
        cols = columns(name)
        return remote(h3.at[:, cols], q3.at[:, cols], x_peer, NAMES.index(name), 12)

    def begin(name):
        if name[0] == "c":
            x_copy(name).start()
        else:
            ring_begin(name, 0)

    def serve(event, name):
        cols = columns(name)
        if event == "cx":
            x_copy(name).wait_recv()
            own = held(name, x_hi * 448, 448)[...]
            cx[:, cols] = (own.astype(F32) + cx[:, cols].astype(F32)).astype(BF)
            ring_begin(name, 0)
        elif event == "m0":
            ring_middle(name, 0)
        elif event == "s":
            sums = ring_total(name, 0)
            for k in range(4):
                if name[0] == "c":
                    for half in range(2):
                        block = sums[half][28 * k:28 * k + 28]
                        zeros = jnp.zeros((4, block.shape[1]), F32)
                        hc[k, :, columns(name, half)] = jnp.concatenate([block, zeros], axis=0).astype(BF)
                else:
                    block = sums[k // 2][(k % 2) * 56:(k % 2 + 1) * 56]
                    zeros = jnp.zeros((8, block.shape[1]), F32)
                    h2[k, :, cols] = jnp.concatenate([block, zeros], axis=0).astype(BF)
            ring_begin(name, 1)
        elif event == "m1":
            ring_middle(name, 1)
        elif event == "t":
            sums = ring_total(name, 1)
            if name[0] == "c":
                for half in range(2):
                    at = columns(name, half)
                    sums_ref[:28, pl.ds(COLS_AB + at.start, at.size)] = sums[half][:28]
            else:
                whole = jnp.concatenate(sums, axis=0)
                first, last = whole[:32], whole[28:60]
                upper = x_hi == 1
                h3[:, cols] = jnp.where(upper, first, last).astype(BF)
                sums_ref[:28, cols] = jnp.where(upper, last, first)[:28]
                x_copy(name).start()
        else:
            x_copy(name).wait_recv()
            sums_ref[:28, cols] = sums_ref[:28, cols] + q3[:, cols].astype(F32)[:28]

    small_peers = [
        along(0, 1 + 2 * (y % 2)), along(0, 3 - 2 * (y % 2)),
        along(1, 1 + 2 * (z % 2)), along(1, 3 - 2 * (z % 2)), x_peer, {"tensor": other},
    ]

    def small_copy(k):
        return pltpu.make_async_remote_copy(
            src_ref=small_in.at[0, k], dst_ref=small_in.at[1, k], send_sem=small_send.at[k], recv_sem=small_recv.at[k],
            device_id=small_peers[k], device_id_type=MESH)

    def small_step(k):
        if k > 0:
            small_copy(k - 1).wait_recv()
            total = small_in[0, k - 1] + small_in[1, k - 1]
            if k < 6:
                small_in[0, k] = total
            else:
                sums_ref[32:40, :D] = total
        if k < 6:
            small_copy(k).start()

    @pl.when(pipe == 0)
    def _():
        xbuf[:, t] = x_ref[...]

    @pl.when(pipe == 1)
    def _():
        gbuf[:, t] = cot_ref[...]
        share_g.start()

    wq[pl.ds(QW, 64), :] = jnp.zeros((64, D), BF)
    wo[pl.ds(QW, 64), :] = jnp.zeros((64, D), BF)
    slot = lax.broadcasted_iota(jnp.int32, (CAP, CAP), 0)
    lane = lax.broadcasted_iota(jnp.int32, (CAP, CAP), 1)
    for m in range(MICRO):
        end = 0
        seg_row = jnp.zeros((CAP, CAP), jnp.int32)
        seg_col = jnp.zeros((CAP, CAP), jnp.int32)
        start = jnp.zeros((CAP, CAP), jnp.int32)
        for s in range(SEQS):
            end = end + len_ref[m, s]
            passed = slot >= end
            seg_row = seg_row + passed.astype(jnp.int32)
            seg_col = seg_col + (lane >= end).astype(jnp.int32)
            start = jnp.where(passed, end, start)
        allow[m] = jnp.where((seg_row == seg_col) & (lane <= slot), 1.0, 0.0)
        cs[m, 2] = jnp.where((seg_row < SEQS) | (pipe == 0), 1.0, 0.0)
        one_hot = jnp.where(slot - start == lane, 1.0, 0.0).astype(BF)
        table = nn(one_hot, tab_ref[...])
        cs[m, 0] = table[:, :128] + table[:, 128:256] + table[:, 256:384]
        cs[m, 1] = table[:, 384:512] + table[:, 512:640] + table[:, 640:768]
    bias_q = jnp.concatenate([bq_ref[...].astype(F32), jnp.zeros((1, 64), F32)], axis=1)
    bias_kv = bkv_ref[...].astype(F32)
    gain_1 = g1_ref[...].astype(F32)
    gain_2 = g2_ref[...].astype(F32)

    @pl.when(pipe == 1)
    def _():
        pass_x.wait_recv()

    share_x.start()
    share_x.wait()
    stream = xbuf[...].astype(F32).reshape(ROWS, D)
    inv = lax.rsqrt(jnp.mean(stream * stream, axis=-1, keepdims=True) + EPS)
    n1[...] = (stream * inv * gain_1).astype(BF)
    loads[0].wait()
    loads[1].wait()
    half_lane = lax.broadcasted_iota(jnp.int32, (CAP, 128), 1)
    for m in range(MICRO):
        rows = pl.ds(m * CAP, CAP)
        qs = nt(n1[rows, :], wq[...]) + bias_q
        vk = pltpu.roll(nn(n1[rows, :], wkv[...]) + bias_kv, 64, 1)
        for j in range(4):
            block = qs[:, j * 128:(j + 1) * 128]
            if j == 3:
                block = jnp.where(half_lane < 64, block, vk)
            block = block * cs[m, 0] + turn(block, half_lane) * cs[m, 1]
            qb[m, j] = block.astype(BF)
            if j == 3:
                odd = jnp.where(half_lane >= 64, block, 0.0)
                kb[m, 1] = odd.astype(BF)
                kb[m, 0] = pltpu.roll(odd, 64, 1).astype(BF)
        even = jnp.where(half_lane < 64, vk, 0.0)
        vb[m, 0] = even.astype(BF)
        vb[m, 1] = pltpu.roll(even, 64, 1).astype(BF)
    for m in range(MICRO):
        q_even = qb[m].reshape(4 * CAP, 128)
        q_odd = qb[m, :3].reshape(3 * CAP, 128)
        seen = allow[m] > 0.0
        mixed = []
        for parity, queries, count in ((0, q_even, 4), (1, q_odd, 3)):
            scores = nt(queries, kb[m, parity]).reshape(count, CAP, CAP) * HEAD ** (-0.5)
            scores = jnp.where(seen[None], scores, -1e30)
            top = jnp.max(scores, axis=-1, keepdims=True)
            grown = jnp.exp(scores - top)
            p = grown * (1.0 / jnp.sum(grown, axis=-1, keepdims=True))
            pmat[m, pl.ds(4 * parity, count)] = p
            mixed.append(nn(p.reshape(count * CAP, CAP).astype(BF), vb[m, parity]))
        for j in range(4):
            block = mixed[0][j * CAP:(j + 1) * CAP]
            if j < 3:
                block = block + mixed[1][j * CAP:(j + 1) * CAP]
            mix[pl.ds(m * CAP, CAP), j * 128:(j + 1) * 128] = block.astype(BF)
    loads[2].wait()
    for c, w in WIDE:
        e1s[:, c:c + w] = nn(mix[...], wo[:, c:c + w]).astype(BF)
    swap_1.start()
    swap_1.wait()
    mid = stream + (e1s[...].astype(F32) + e1r[...].astype(F32))
    middle[...] = mid.reshape(MICRO, 2, OWN, D)
    inv = lax.rsqrt(jnp.mean(mid * mid, axis=-1, keepdims=True) + EPS)
    n2[...] = (mid * inv * gain_2).astype(BF)
    loads[3].wait()
    for c, w in TILES:
        g = nn(n2[...], wgu[0, :, c:c + w])
        u = nn(n2[...], wgu[1, :, c:c + w])
        sig = jax.nn.sigmoid(g)
        silu = g * sig
        hidden[:, c:c + w] = (silu * u).astype(BF)
        dup[:, c:c + w] = silu.astype(BF)
        dgate[:, c:c + w] = (u * sig * (1.0 + g * (1.0 - sig))).astype(BF)
    loads[4].wait()
    for c, w in WIDE:
        part[:, :, :, c:c + w] = nn(hidden[...], wd[:, c:c + w]).reshape(MICRO, 2, OWN, w)
    e2s[...] = part[:, other].astype(BF)
    swap_2.start()
    swap_2.wait()
    pipe_out[...] = (middle[:, t] + (part[:, t] + e2r[...].astype(F32))).astype(BF)
    rows_ref[0] = pipe_out[...].astype(F32)

    def reordered(turned):
        return jnp.concatenate(
            [turned[(4 * b + a) * 56:(4 * b + a + 1) * 56] for a in range(4) for b in range(4)], axis=0).astype(BF)

    def weights_down():
        rows = gbuf[...].reshape(ROWS, D)
        turned = nt(perm[...], rows)
        for name, order in (("a0", 0), ("b0", 1), ("c0", 2), ("c1", 2)):
            if name != "c1":
                lt[order] = (
                    turned.astype(BF) if order == 0 else reordered(turned) if order == 1 else rows.astype(F32).T.astype(BF))
            _, c, w, _ = PIECES[name]
            gdown[:, c:c + w] = nn(lt[order], hidden[:, c:c + w]).astype(BF)
            begin(name)

    def weights_gate_up():
        for name, order in (("a1", 0), ("b1", 1), ("c2", 2), ("a2", 0), ("b2", 1), ("c3", 2)):
            buf, c, w, _ = PIECES[name]
            which, rhs = ((0, dgate), (1, dup))[buf == "up"]
            wgu[which, :, c:c + w] = nn(lt_n[order], rhs[:, c:c + w]).astype(BF)
            begin(name)

    def weights_out():
        lt[0] = nt(perm[...], mb_ref[...]).astype(BF)
        gout[...] = nn(lt[0], mix[...]).astype(BF)
        begin("a3")

    def norm_back(grads, values, gain):
        inverse = lax.rsqrt(jnp.mean(values * values, axis=-1, keepdims=True) + EPS)
        scaled = values * inverse
        weighted = grads * gain
        back = inverse * (weighted - scaled * jnp.mean(weighted * scaled, axis=-1, keepdims=True))
        return back, grads * scaled

    loads[5].wait()

    def backward(turn_now, _):
        chain = pl.when(turn_now == 0)
        weights = pl.when(turn_now == pipe)

        @chain
        def _():
            @pl.when(pipe == 0)
            def _():
                pass_x.start()

        @weights
        def _():
            turned = nt(perm[...], n2[...])
            lt_n[0] = turned.astype(BF)
            lt_n[1] = reordered(turned)
            lt_n[2] = n2[...].astype(F32).T.astype(BF)

        @chain
        def _():
            @pl.when(pipe == 0)
            def _():
                pass_g.wait_recv()
                share_g.start()

            share_g.wait()
            for m in range(MICRO):
                live = cs[m, 2][:, :1].astype(BF).reshape(2, OWN, 1)
                gbuf[m] = gbuf[m] * live

        weights(weights_down)

        @chain
        def _():
            grad = gbuf[...].reshape(ROWS, D)
            for c, w in TILES:
                gh = nt(grad, wd[c:c + w, :])
                dgate[:, c:c + w] = (gh * dgate[:, c:c + w].astype(F32)).astype(BF)
                dup[:, c:c + w] = (gh * dup[:, c:c + w].astype(F32)).astype(BF)
            for c, w in WIDE:
                e1s[:, c:c + w] = (nt(dgate[...], wgu[0, c:c + w, :]) + nt(dup[...], wgu[1, c:c + w, :])).astype(BF)
            swap_3.start()

        weights(weights_gate_up)

        @chain
        def _():
            swap_3.wait()
            grads = e1s[...].astype(F32) + e1r[...].astype(F32)
            back, terms = norm_back(grads, middle[...].reshape(ROWS, D), gain_2)
            row = lax.broadcasted_iota(jnp.int32, (ROWS, 1), 0)
            mine = ((row >> 6) & 1) == t
            small_in[0, 0] = jnp.zeros((8, D), F32)
            small_in[0, 0, 1:2, :] = jnp.sum(jnp.where(mine, terms, 0.0), axis=0, keepdims=True)
            grad_mid = gbuf[...].reshape(ROWS, D).astype(F32) + back
            gmid[...] = grad_mid.reshape(MICRO, 2, OWN, D)
            mb_ref[...] = grad_mid.astype(BF)

        weights(weights_out)
        chain(attention_back)
        return 0

    def attention_back():
        gmix = nt(mb_ref[...], wo[...]).astype(BF)
        for m in range(MICRO):
            blocks = [gmix[m * CAP:(m + 1) * CAP, j * 128:(j + 1) * 128] for j in range(4)]
            q_even = qb[m].reshape(4 * CAP, 128)
            q_odd = qb[m, :3].reshape(3 * CAP, 128)
            out = []
            for parity, queries, count in ((0, q_even, 4), (1, q_odd, 3)):
                gm = jnp.concatenate(blocks[:count], axis=0)
                p = pmat[m, pl.ds(4 * parity, count)].reshape(count * CAP, CAP)
                gp = nt(gm, vb[m, parity])
                ds = (p * (gp - jnp.sum(p * gp, axis=-1, keepdims=True))).astype(BF)
                out.append((nn(ds, kb[m, parity]), tn(ds, queries), tn(p.astype(BF), gm)))
            keys = pltpu.roll(out[0][1], 64, 1) + out[1][1]
            values = out[0][2] + pltpu.roll(out[1][2], 64, 1)
            rows = pl.ds(m * CAP, CAP)
            for j in range(4):
                block = out[0][0][j * CAP:(j + 1) * CAP]
                if j < 3:
                    block = block + out[1][0][j * CAP:(j + 1) * CAP]
                else:
                    block = jnp.where(half_lane < 64, block, keys)
                block = block * HEAD ** (-0.5)
                block = block * cs[m, 0] - turn(block, half_lane) * cs[m, 1]
                if j == 3:
                    gqkv[rows, 512:640] = pltpu.roll(jnp.where(half_lane < 64, values, block), 64, 1).astype(BF)
                    block = jnp.where(half_lane < 64, block, 0.0)
                gqkv[rows, j * 128:(j + 1) * 128] = block.astype(BF)
        for c, w in WIDE:
            part[:, :, :, c:c + w] = (
                nn(gqkv[:, :512], wq[:, c:c + w]) + nt(gqkv[:, 512:], wkv[c:c + w, :])).reshape(MICRO, 2, OWN, w)
        e2s[...] = part[:, other].astype(BF)
        swap_4.start()
        swap_4.wait()
        grads = (part[:, t] + e2r[...].astype(F32)).reshape(MICRO * OWN, D)
        back, terms = norm_back(grads, xbuf[:, t].astype(F32).reshape(MICRO * OWN, D), gain_1)
        total = gmid[:, t] + back.reshape(MICRO, OWN, D)
        rows_ref[1] = total

        @pl.when(pipe == 0)
        def _():
            pass_x.wait_send()

        pipe_out[...] = total.astype(BF)

        @pl.when(pipe == 1)
        def _():
            pass_g.start()

        small_in[0, 0, 0:1, :] = jnp.sum(terms, axis=0, keepdims=True)
        bias = jnp.sum(gqkv[...].astype(F32), axis=0, keepdims=True)
        wide = jnp.concatenate([bias[:, :512], jnp.zeros((1, D - 512), F32)], axis=1)
        small_in[0, 0, 2:3, :] = jnp.where(t == 0, wide, pltpu.roll(wide, QW, 1))
        for c in range(2):
            small_in[0, 0, 3 + c:4 + c, :128] = jnp.where(t == c, bias[:, 512:], 0.0)

    lax.fori_loop(0, 2, backward, 0)
    lt[1] = nt(perm[...], n1[...]).astype(BF)
    gqkv_w[...] = nn(lt[1], gqkv[...]).astype(BF)
    begin("a4")

    for step, event in enumerate(SERVICE):
        if step % 4 == 0 and step < 28:
            small_step(step // 4)
        serve(*event.split(":"))
    for name in NAMES:
        for stage in range(2):
            for k in range(6):
                ring_copy(name, stage, k).wait_send()
        x_copy(name).wait_send()
    for k in range(6):
        small_copy(k).wait_send()

    @pl.when(pipe == 1)
    def _():
        pass_g.wait_send()


def run_train(lens, x, cot, g1, g2, bq, bkv, wq, wkv, wo, wgu, wd):
    vmem = pl.BlockSpec(memory_space=VMEM)
    hbm = pl.BlockSpec(memory_space=pl.ANY)
    dma = pltpu.SemaphoreType.DMA
    return pl.pallas_call(
        train_kernel,
        out_shape=(
            jax.ShapeDtypeStruct((40, COLS_AB + COLS_C), F32),
            jax.ShapeDtypeStruct((2, MICRO, OWN, D), F32),
        ),
        in_specs=[pl.BlockSpec(memory_space=pltpu.SMEM)] + [vmem] * 7 + [hbm] * 6,
        out_specs=(vmem,) * 2,
        scratch_shapes=[
            VMEM((512, D), BF), VMEM((D, 128), BF), VMEM((512, D), BF), VMEM((2, D, FH), BF), VMEM((FH, D), BF), VMEM((D, D), BF),
            VMEM((MICRO, 2, OWN, D), BF), VMEM((MICRO, 2, OWN, D), BF),
            VMEM((ROWS, D), BF), VMEM((ROWS, D), BF),
            VMEM((MICRO, OWN, D), BF), VMEM((MICRO, OWN, D), BF), VMEM((MICRO, OWN, D), BF),
            VMEM((ROWS, D), BF), VMEM((ROWS, D), BF),
            VMEM((MICRO, 4, CAP, 128), BF), VMEM((MICRO, 2, CAP, 128), BF), VMEM((MICRO, 2, CAP, 128), BF),
            VMEM((MICRO, 7, CAP, CAP), F32), VMEM((ROWS, 512), BF), VMEM((MICRO, 2, OWN, D), F32),
            VMEM((ROWS, FH), BF), VMEM((ROWS, FH), BF), VMEM((ROWS, FH), BF),
            VMEM((3, D, ROWS), BF), VMEM((MICRO, 2, OWN, D), F32), VMEM((MICRO, 2, OWN, D), F32),
            VMEM((MICRO, 3, CAP, 128), F32), VMEM((MICRO, CAP, CAP), F32), VMEM((ROWS, 640), BF),
            VMEM((3, D, ROWS), BF), VMEM((ROWS, D), BF), VMEM((D, FH), BF), VMEM((D, 512), BF), VMEM((D, 640), BF),
            VMEM((2, 112, COLS_AB), BF), VMEM((2, 2, 112, COLS_AB), BF),
            VMEM((4, 64, COLS_AB), BF), VMEM((2, 32, COLS_AB), BF), VMEM((2, 2, 32, COLS_AB), BF),
            VMEM((32, COLS_AB), BF), VMEM((32, COLS_AB), BF),
            VMEM((448, COLS_C), BF), VMEM((112, COLS_C), BF), VMEM((2, 112, COLS_C), BF),
            VMEM((4, 32, COLS_C), BF), VMEM((32, COLS_C), BF), VMEM((2, 32, COLS_C), BF),
            VMEM((2, 6, 8, D), F32),
            dma((6,)), dma((8,)), dma((8,)), dma((len(NAMES), 13)), dma((len(NAMES), 13)), dma((6,)), dma((6,)),
        ],
        compiler_params=pltpu.CompilerParams(collective_id=0, has_side_effects=True, vmem_limit_bytes=63 * MIB),
        name="train",
    )(lens, x, cot, g1, g2, bq, bkv, jnp.asarray(rope_table()), wq, wkv, wo, wgu, wd, jnp.asarray(row_order()))


def place_kernel(
    sums_ref, rows_ref,
    so_ref, ig_ref, gain1_ref, gq_ref, bq_ref, gkv_ref, bkv_ref, go_ref, gain2_ref, ggu_ref, gd_ref,
):
    so_ref[...] = rows_ref[0].astype(BF)
    ig_ref[...] = rows_ref[1]
    gain1_ref[...] = sums_ref[32:33, :D]
    gain2_ref[...] = sums_ref[33:34, :D]
    bq_ref[...] = sums_ref[34:35, :D]
    bkv_ref[...] = sums_ref[35:37, :128]
    gq_ref[:, 0, :] = sums_ref[:28, 3200:3200 + QW]
    gkv_ref[:, 0, :] = sums_ref[:28, 3712:3840]
    go_ref[:, 0, :] = sums_ref[:28, 2688:2688 + QW]
    for ref, names in ((gd_ref.at[:, 0], "a0 b0 c0 c1"), (ggu_ref.at[:, 0], "a1 a2 c2"), (ggu_ref.at[:, 1], "b1 b2 c3")):
        for name in names.split():
            _, c, w, at = PIECES[name]
            at = at + COLS_AB * (name[0] == "c")
            ref[:, c:c + w] = sums_ref[:28, at:at + w]


def run_place(*arrays):
    vmem = pl.BlockSpec(memory_space=VMEM)
    shapes = (
        (MICRO, OWN, D), (MICRO, OWN, D), (1, D), (28, 1, QW), (1, D), (28, 1, 128), (2, 128),
        (28, 1, QW), (1, D), (28, 2, FH), (28, 1, FH),
    )
    return pl.pallas_call(
        place_kernel,
        out_shape=tuple(jax.ShapeDtypeStruct(s, F32 if i else BF) for i, s in enumerate(shapes)),
        in_specs=[vmem] * 2,
        out_specs=(vmem,) * 11,
        compiler_params=pltpu.CompilerParams(vmem_limit_bytes=32 * MIB),
        name="place",
    )(*arrays)


def body(
    inputs, cotangent, lengths, gain_attn, w_query, b_query, w_keyval, b_keyval, w_out, gain_mlp, w_gate_up, w_down,
):
    outs = run_train(
        lengths[:, 0], inputs, cotangent, gain_attn, gain_mlp, b_query, b_keyval[0],
        jnp.swapaxes(w_query[0], 0, 1), w_keyval[0, :, 0], w_out[0],
        jnp.swapaxes(w_gate_up[0], 0, 1), w_down[0],
    )
    so, ig, gain1, gq, bq, gkv, bkv, go, gain2, ggu, gd = run_place(*outs)
    return (
        so[None], ig[None], gain1, jnp.swapaxes(gq, 0, 1), bq, gkv[None], bkv[None],
        jnp.transpose(go, (1, 2, 0)), gain2, ggu[None], jnp.transpose(gd, (1, 2, 0)),
    )


def solution(mesh):
    placed = (
        P(None, ("dp", "tensor"), None),
        P(None, ("dp", "tensor"), None),
        P(None, "dp", None),
        P("pipe", None),
        P("pipe", None, "tensor"),
        P("pipe", "tensor"),
        P("pipe", None, "tensor", None),
        P("pipe", "tensor", None),
        P("pipe", "tensor", None),
        P("pipe", None),
        P("pipe", None, None, "tensor"),
        P("pipe", "tensor", None),
    )
    return jax.shard_map(
        body,
        mesh=mesh,
        in_specs=placed,
        out_specs=(
            P("pipe", None, ("dp", "tensor"), None),
            P("pipe", None, ("dp", "tensor"), None),
            P("pipe", None),
            P("pipe", "dp", "tensor"),
            P("pipe", None),
            P("pipe", "dp", "tensor", None),
            P("pipe", None, None),
            P("pipe", "tensor", "dp"),
            P("pipe", None),
            P("pipe", "dp", None, "tensor"),
            P("pipe", "tensor", "dp"),
        ),
        check_vma=False,
    )
```

profile of v0, /device:TPU:0, one launch (start us, length us, event | category | flops | bytes accessed | tf_op | source)
XLA Modules:
  0.0 163.8 jit_solution(2195840566971372460)
XLA Ops:
  0.6 7.9 %copy.27 = bf16[1,896,2,2432]{3,1,2,0:T(8,128)(2,1)} copy(bf16[1,896,2,2432]{3,2,1,0:T(2,128)(2,1)} %param.24) | data formatting | bytes 17432576 | tf_op args[10]
  8.5 151.4 %train.1 = (f32[40,8448]{1,0:T(8,128)}, f32[2,2,64,896]{3,2,1,0:T(8,128)}) custom-call(s32[2,4]{1,0:T(2,128)} %bitcast.26, bf16[2,64,896]{2,1,0:T(8,128)(2,1)} %x_ref.1, bf16[2,64,896]{2,1,0:T(8,128)(2,1)} %cot_ref.1, bf16[1,896]{1,0:T(2,128)(2,1)} %g1_ref.1, bf16[1,896]{1,0:T(2,128)(2,1)} %g2_ref.1, bf16[1,448]{1,0:T(2,128)(2,1)} %bq_ref.1, ...), custom_call_target="tpu_custom_call" | custom-call | tf_op jit(solution)/shard_map/train/pallas_call | solution.py:597
  160.0 0.0 copy-start
  160.0 1.3 copy-done
  161.3 0.0 copy-start.1
  161.3 1.2 copy-done.1
  162.5 1.3 place.1
Async XLA Ops:
  160.0 1.3 copy-start
  161.3 1.2 copy-start.1
where the time goes:
time: 164 us
  Pallas kernels  153 us (93%)
  local copies, waits for them, and re-layouts  10.4 us (6%)
    pallas_call x1, Pallas kernels, run_train(): pl.pallas_call(train_kernel, out_shape=(jax.ShapeDtypeStruct((40, COLS_AB...  151 us
    unnamed x5, local copies, waits for them, and re-layouts  10.4 us

commit v1 on v0

--- a/solution.py
+++ b/solution.py
@@ -138,9 +138,9 @@
             src_ref=src, dst_ref=dst, send_sem=send_sem.at[i], recv_sem=recv_sem.at[i],
             device_id={"pipe": 1 - pipe}, device_id_type=MESH)
 
-    share_x = to_core(xbuf.at[:, t], xbuf.at[:, t], 0)
+    share_x = [to_core(xbuf.at[m, t], xbuf.at[m, t], 8 * m) for m in range(MICRO)]
     share_g = to_core(gbuf.at[:, t], gbuf.at[:, t], 1)
-    pass_x = to_pipe(pipe_out, xbuf.at[:, t], 2)
+    pass_x = [to_pipe(pipe_out.at[m], xbuf.at[m, t], 2 + 7 * m) for m in range(MICRO)]
     pass_g = to_pipe(pipe_out, gbuf.at[:, t], 3)
     swap_1 = to_core(e1s, e1r, 4)
     swap_2 = to_core(e2s, e2r, 5)
@@ -331,7 +331,7 @@
             seg_col = seg_col + (lane >= end).astype(jnp.int32)
             start = jnp.where(passed, end, start)
         allow[m] = jnp.where((seg_row == seg_col) & (lane <= slot), 1.0, 0.0)
-        cs[m, 2] = jnp.where((seg_row < SEQS) | (pipe == 0), 1.0, 0.0)
+        cs[m, 2] = jnp.where(seg_row < SEQS, 1.0, 0.0)
         one_hot = jnp.where(slot - start == lane, 1.0, 0.0).astype(BF)
         table = nn(one_hot, tab_ref[...])
         cs[m, 0] = table[:, :128] + table[:, 128:256] + table[:, 256:384]
@@ -343,18 +343,27 @@
 
     @pl.when(pipe == 1)
     def _():
-        pass_x.wait_recv()
-
-    share_x.start()
-    share_x.wait()
-    stream = xbuf[...].astype(F32).reshape(ROWS, D)
-    inv = lax.rsqrt(jnp.mean(stream * stream, axis=-1, keepdims=True) + EPS)
-    n1[...] = (stream * inv * gain_1).astype(BF)
-    loads[0].wait()
-    loads[1].wait()
+        share_g.wait()
+        for m in range(MICRO):
+            gbuf[m] = gbuf[m] * cs[m, 2][:, :1].astype(BF).reshape(2, OWN, 1)
+        loads[4].wait()
+        for c, w in TILES:
+            gdown[:ROWS, c:c + w] = nt(gbuf[...].reshape(ROWS, D), wd[c:c + w, :]).astype(BF)
+
     half_lane = lax.broadcasted_iota(jnp.int32, (CAP, 128), 1)
-    for m in range(MICRO):
+
+    def arrived(m):
+        @pl.when(pipe == 1)
+        def _():
+            pass_x[m].wait_recv()
+            share_x[m].start()
+
+    def projections(m):
+        share_x[m].wait()
         rows = pl.ds(m * CAP, CAP)
+        stream = xbuf[m].astype(F32).reshape(CAP, D)
+        inv = lax.rsqrt(jnp.mean(stream * stream, axis=-1, keepdims=True) + EPS)
+        n1[rows, :] = (stream * inv * gain_1).astype(BF)
         qs = nt(n1[rows, :], wq[...]) + bias_q
         vk = pltpu.roll(nn(n1[rows, :], wkv[...]) + bias_kv, 64, 1)
         for j in range(4):
@@ -370,7 +379,8 @@
         even = jnp.where(half_lane < 64, vk, 0.0)
         vb[m, 0] = even.astype(BF)
         vb[m, 1] = pltpu.roll(even, 64, 1).astype(BF)
-    for m in range(MICRO):
+
+    def attention(m):
         q_even = qb[m].reshape(4 * CAP, 128)
         q_odd = qb[m, :3].reshape(3 * CAP, 128)
         seen = allow[m] > 0.0
@@ -388,12 +398,26 @@
             if j < 3:
                 block = block + mixed[1][j * CAP:(j + 1) * CAP]
             mix[pl.ds(m * CAP, CAP), j * 128:(j + 1) * 128] = block.astype(BF)
+
+    @pl.when(pipe == 0)
+    def _():
+        share_x[0].start()
+        share_x[1].start()
+
+    loads[0].wait()
+    loads[1].wait()
+    arrived(0)
+    projections(0)
+    arrived(1)
+    attention(0)
+    projections(1)
+    attention(1)
     loads[2].wait()
     for c, w in WIDE:
         e1s[:, c:c + w] = nn(mix[...], wo[:, c:c + w]).astype(BF)
     swap_1.start()
     swap_1.wait()
-    mid = stream + (e1s[...].astype(F32) + e1r[...].astype(F32))
+    mid = xbuf[...].astype(F32).reshape(ROWS, D) + (e1s[...].astype(F32) + e1r[...].astype(F32))
     middle[...] = mid.reshape(MICRO, 2, OWN, D)
     inv = lax.rsqrt(jnp.mean(mid * mid, axis=-1, keepdims=True) + EPS)
     n2[...] = (mid * inv * gain_2).astype(BF)
@@ -406,7 +430,11 @@
         hidden[:, c:c + w] = (silu * u).astype(BF)
         dup[:, c:c + w] = silu.astype(BF)
         dgate[:, c:c + w] = (u * sig * (1.0 + g * (1.0 - sig))).astype(BF)
-    loads[4].wait()
+
+    @pl.when(pipe == 0)
+    def _():
+        loads[4].wait()
+
     for c, w in WIDE:
         part[:, :, :, c:c + w] = nn(hidden[...], wd[:, c:c + w]).reshape(MICRO, 2, OWN, w)
     e2s[...] = part[:, other].astype(BF)
@@ -459,7 +487,8 @@
         def _():
             @pl.when(pipe == 0)
             def _():
-                pass_x.start()
+                pass_x[0].start()
+                pass_x[1].start()
 
         @weights
         def _():
@@ -474,21 +503,26 @@
             def _():
                 pass_g.wait_recv()
                 share_g.start()
-
-            share_g.wait()
-            for m in range(MICRO):
-                live = cs[m, 2][:, :1].astype(BF).reshape(2, OWN, 1)
-                gbuf[m] = gbuf[m] * live
+                share_g.wait()
 
         weights(weights_down)
 
         @chain
         def _():
-            grad = gbuf[...].reshape(ROWS, D)
-            for c, w in TILES:
-                gh = nt(grad, wd[c:c + w, :])
+            def scale(c, w, gh):
                 dgate[:, c:c + w] = (gh * dgate[:, c:c + w].astype(F32)).astype(BF)
                 dup[:, c:c + w] = (gh * dup[:, c:c + w].astype(F32)).astype(BF)
+
+            @pl.when(pipe == 0)
+            def _():
+                for c, w in TILES:
+                    scale(c, w, nt(gbuf[...].reshape(ROWS, D), wd[c:c + w, :]))
+
+            @pl.when(pipe == 1)
+            def _():
+                for c, w in TILES:
+                    scale(c, w, gdown[:ROWS, c:c + w].astype(F32))
+
             for c, w in WIDE:
                 e1s[:, c:c + w] = (nt(dgate[...], wgu[0, c:c + w, :]) + nt(dup[...], wgu[1, c:c + w, :])).astype(BF)
             swap_3.start()
@@ -553,7 +587,8 @@
 
         @pl.when(pipe == 0)
         def _():
-            pass_x.wait_send()
+            pass_x[0].wait_send()
+            pass_x[1].wait_send()
 
         pipe_out[...] = total.astype(BF)
 
@@ -620,7 +655,7 @@
             VMEM((448, COLS_C), BF), VMEM((112, COLS_C), BF), VMEM((2, 112, COLS_C), BF),
             VMEM((4, 32, COLS_C), BF), VMEM((32, COLS_C), BF), VMEM((2, 32, COLS_C), BF),
             VMEM((2, 6, 8, D), F32),
-            dma((6,)), dma((8,)), dma((8,)), dma((len(NAMES), 13)), dma((len(NAMES), 13)), dma((6,)), dma((6,)),
+            dma((6,)), dma((10,)), dma((10,)), dma((len(NAMES), 13)), dma((len(NAMES), 13)), dma((6,)), dma((6,)),
         ],
         compiler_params=pltpu.CompilerParams(collective_id=0, has_side_effects=True, vmem_limit_bytes=63 * MIB),
         name="train",
@@ -658,7 +693,7 @@
         out_shape=tuple(jax.ShapeDtypeStruct(s, F32 if i else BF) for i, s in enumerate(shapes)),
         in_specs=[vmem] * 2,
         out_specs=(vmem,) * 11,
-        compiler_params=pltpu.CompilerParams(vmem_limit_bytes=32 * MIB),
+        compiler_params=pltpu.CompilerParams(vmem_limit_bytes=60 * MIB),
         name="place",
     )(*arrays)
 

time: 164 us -> 161 us (0.982)
  local copies, waits for them, and re-layouts: 10.4 us -> 7.87 us
    unnamed x5 -> x1, local copies, waits for them, and re-layouts: 10.4 us -> 7.87 us
    pallas_call x1, Pallas kernels: 151 us -> 149 us  [run_train(): pl.pallas_call(train_kernel, out_shape=(jax.ShapeDtypeStruct((40, COLS_AB...]
where the time goes in v1:
time: 161 us
  Pallas kernels  152 us (94%)
  local copies, waits for them, and re-layouts  7.87 us (5%)
    pallas_call x1, Pallas kernels, run_train(): pl.pallas_call(train_kernel, out_shape=(jax.ShapeDtypeStruct((40, COLS_AB...  149 us
    unnamed x1, local copies, waits for them, and re-layouts  7.87 us

profile of v1, /device:TPU:0, one launch (start us, length us, event | category | flops | bytes accessed | tf_op | source)
XLA Modules:
  0.0 160.9 jit_solution(15526777935295608450)
XLA Ops:
  0.6 7.9 %copy.27 = bf16[1,896,2,2432]{3,1,2,0:T(8,128)(2,1)} copy(bf16[1,896,2,2432]{3,2,1,0:T(2,128)(2,1)} %param.24) | data formatting | bytes 17432576 | tf_op args[10]
  8.5 149.5 %train.1 = (f32[40,8448]{1,0:T(8,128)}, f32[2,2,64,896]{3,2,1,0:T(8,128)}) custom-call(s32[2,4]{1,0:T(2,128)} %bitcast.26, bf16[2,64,896]{2,1,0:T(8,128)(2,1)} %x_ref.1, bf16[2,64,896]{2,1,0:T(8,128)(2,1)} %cot_ref.1, bf16[1,896]{1,0:T(2,128)(2,1)} %g1_ref.1, bf16[1,896]{1,0:T(2,128)(2,1)} %g2_ref.1, bf16[1,448]{1,0:T(2,128)(2,1)} %bq_ref.1, ...), custom_call_target="tpu_custom_call" | custom-call | tf_op jit(solution)/shard_map/train/pallas_call | solution.py:632
  158.0 2.8 %place.1 = (bf16[2,64,896]{2,1,0:T(8,128)(2,1)}, f32[2,64,896]{2,1,0:T(8,128)}, f32[1,896]{1,0:T(1,128)}, f32[28,1,448]{2,1,0:T(1,128)}, f32[1,896]{1,0:T(1,128)...) custom-call(f32[40,8448]{1,0:T(8,128)} %get-tuple-element.24.sums_re, ...), custom_call_target="tpu_custom_call" | custom-call | tf_op jit(solution)/shard_map/place/pallas_call | solution.py:691

commit v2 on v1

--- a/solution.py
+++ b/solution.py
@@ -40,19 +40,19 @@
 SERVICE = (
     "cx:c0 m0:a0 m0:a1 m0:b0",
     "m0:b1 m0:a2 m0:b2 m0:a3",
-    "m0:c0 cx:c1 s:b0 m0:a4",
-    "s:b1 cx:c2 s:a0 s:b2",
-    "s:a1 s:c0 cx:c3 m0:c1",
-    "m0:c2 s:a2 m1:a0 s:a3",
-    "m1:a1 m1:b0 m0:c3 s:c1",
-    "s:a4 s:c2 m1:b1 m1:a2",
-    "m1:b2 t:a0 m1:a3 m1:c0",
-    "t:a1 t:b0 e:a0 s:c3",
-    "m1:c1 m1:a4 m1:c2 t:b1",
-    "e:a1 t:a2 t:a3 e:b0",
-    "t:b2 t:c0 m1:c3 t:a4",
-    "t:c1 t:c2 e:b1 t:c3",
-    "e:a2 e:a3 e:b2 e:a4",
+    "m0:c0 s:b0 cx:c1 m0:a4",
+    "s:b1 s:a0 s:b2 s:a1",
+    "s:c0 cx:c2 m0:c1 m1:a0",
+    "s:a2 m1:a1 s:a3 cx:c3",
+    "m0:c2 m1:b0 s:c1 t:a0",
+    "s:a4 m1:a2 m1:b1 t:a1",
+    "m1:b2 m1:a3 e:a0 m0:c3",
+    "m1:c0 s:c2 t:b0 m1:c1",
+    "m1:a4 e:a1 t:b1 t:a2",
+    "t:a3 t:b2 t:c0 s:c3",
+    "m1:c2 t:c1 e:b0 t:a4",
+    "e:b1 m1:c3 t:c2 e:a2",
+    "e:a3 t:c3 e:b2 e:a4",
 )
 SERVICE = tuple(event for line in SERVICE for event in line.split())
 TILES = ((0, 512), (512, 512), (1024, 512), (1536, 512), (2048, 384))

time: 161 us -> 162 us (level)
  no operation moved by 1% of the time
where the time goes in v2:
time: 162 us
  Pallas kernels  153 us (94%)
  local copies, waits for them, and re-layouts  7.87 us (5%)
    pallas_call x1, Pallas kernels, run_train(): pl.pallas_call(train_kernel, out_shape=(jax.ShapeDtypeStruct((40, COLS_AB...  150 us
    unnamed x1, local copies, waits for them, and re-layouts  7.87 us

profile of v2, /device:TPU:0, one launch (start us, length us, event | category | flops | bytes accessed | tf_op | source)
XLA Modules:
  0.0 161.6 jit_solution(3280442477768146654)
XLA Ops:
  0.6 7.9 %copy.27 = bf16[1,896,2,2432]{3,1,2,0:T(8,128)(2,1)} copy(bf16[1,896,2,2432]{3,2,1,0:T(2,128)(2,1)} %param.24) | data formatting | bytes 17432576 | tf_op args[10]
  8.5 150.2 %train.1 = (f32[40,8448]{1,0:T(8,128)}, f32[2,2,64,896]{3,2,1,0:T(8,128)}) custom-call(s32[2,4]{1,0:T(2,128)} %bitcast.26, bf16[2,64,896]{2,1,0:T(8,128)(2,1)} %x_ref.1, bf16[2,64,896]{2,1,0:T(8,128)(2,1)} %cot_ref.1, bf16[1,896]{1,0:T(2,128)(2,1)} %g1_ref.1, bf16[1,896]{1,0:T(2,128)(2,1)} %g2_ref.1, bf16[1,448]{1,0:T(2,128)(2,1)} %bq_ref.1, ...), custom_call_target="tpu_custom_call" | custom-call | tf_op jit(solution)/shard_map/train/pallas_call | solution.py:632
  158.8 2.8 %place.1 = (bf16[2,64,896]{2,1,0:T(8,128)(2,1)}, f32[2,64,896]{2,1,0:T(8,128)}, f32[1,896]{1,0:T(1,128)}, f32[28,1,448]{2,1,0:T(1,128)}, f32[1,896]{1,0:T(1,128)...) custom-call(f32[40,8448]{1,0:T(8,128)} %get-tuple-element.24.sums_re, ...), custom_call_target="tpu_custom_call" | custom-call | tf_op jit(solution)/shard_map/place/pallas_call | solution.py:691
